TPU v7x, 32 devices: a whole 2x2x4 slice. The times are simulated.
32 devices in a mesh: seq: 8 (over y, x, core), chan: 4 (over z).
Axes of the slice: x: 2, y: 2, z: 4, core: 2. Of those that a mesh axis runs over, the one named last changes fastest.
Arguments:
- doc_ids: int32 [2048], replicated, may hold values from 0 to 3, never falling along the last dimension, each value on 1 to 1024 neighbouring positions
- attn_queries: bfloat16 [2048, 8192], P(('seq', 'chan')), may hold values from -6 to 6
- attn_keys: bfloat16 [2048, 8192], P(('seq', 'chan')), may hold values from -6 to 6
- attn_values: bfloat16 [2048, 8192], P(('seq', 'chan')), may hold values from -6 to 6
- attn_cot: bfloat16 [2048, 8192], P(('seq', 'chan')), may hold values from -6 to 6
Outputs:
- attn_out: bfloat16 [2048, 8192], P('seq', 'chan')
- query_grad: bfloat16 [2048, 8192], P('seq', 'chan')
- key_grad: bfloat16 [2048, 8192], P('seq', 'chan')
- value_grad: bfloat16 [2048, 8192], P('seq', 'chan')
Inputs may be any that keep to these rules, and one draw needn't show every extreme that they name: `doc_ids`: documents are runs of equal ids that never fall; each holds 1 to 1024 tokens and one holds exactly 1024.
All inputs are finite; a program needn't handle non-finite values.
Results may differ from a plain program's by a relative error of at most 0.03.
Values may be sent and summed in bfloat16 or wider, within the bound.
No kernel may reach another device: no remote copies, remote signals or barrier semaphores. Data moves between devices by JAX's collectives and lax.ppermute only.
A program may use at most 256 MiB of HBM per device.

v0:
```python
from functools import reduce

import jax
import jax.numpy as jnp
from jax import lax
from jax.sharding import PartitionSpec as P

HEAD_DIM = 128
SPAN_SH = 4


NEG = -1e30


def shifted(value, axis, by):
    count = lax.axis_size(axis)
    pairs = [(i, i + by) for i in range(count) if 0 <= i + by < count]
    return lax.ppermute(value, axis, pairs)


def guarded(work, operands):
    return work(*operands)


def allowed_pairs(doc_ids, query_shard, key_shard, row_count, shard_total):
    offsets = jnp.arange(row_count, dtype=jnp.int32)
    query_pos = query_shard * row_count + offsets
    key_pos = key_shard * row_count + offsets
    query_doc = lax.dynamic_slice_in_dim(doc_ids, query_shard * row_count, row_count)
    key_doc = lax.dynamic_slice_in_dim(doc_ids, key_shard * row_count, row_count)
    inside = (key_shard >= 0) & (query_shard < shard_total)
    same_doc = key_doc[None, :] == query_doc[:, None]
    return same_doc & (key_pos[None, :] <= query_pos[:, None]) & inside


def attention_layer(doc_ids, shard_index, attn_queries, attn_keys, attn_values, attn_cot):
    query_loc, key_loc, value_loc, cot_loc = (
        lax.all_to_all(attn_queries, "chan", split_axis=1, concat_axis=0, tiled=True),
        lax.all_to_all(attn_keys, "chan", split_axis=1, concat_axis=0, tiled=True),
        lax.all_to_all(attn_values, "chan", split_axis=1, concat_axis=0, tiled=True),
        lax.all_to_all(attn_cot, "chan", split_axis=1, concat_axis=0, tiled=True),
    )
    row_count = query_loc.shape[0]
    head_count = query_loc.shape[1] // HEAD_DIM
    head_shape = (row_count, head_count, HEAD_DIM)
    query_heads = query_loc.reshape(head_shape)
    key_heads = key_loc.reshape(head_shape)
    value_heads = value_loc.reshape(head_shape)
    cot_heads = cot_loc.reshape(head_shape)
    shard_total = lax.axis_size("seq")
    score_scale = HEAD_DIM ** (-0.5)

    def score_block(key_block, pair_mask):
        raw_scores = (
            jnp.einsum("qhe,khe->hqk", query_heads, key_block, preferred_element_type=jnp.float32)
            * score_scale
        )
        return jnp.where(pair_mask[None], raw_scores, NEG)

    def mix_block(weight_block, value_block):
        return jnp.einsum(
            "hqk,khe->qhe", weight_block, value_block, preferred_element_type=jnp.float32
        )

    def weight_grads(value_block):
        return jnp.einsum(
            "qhe,khe->hqk", cot_heads, value_block, preferred_element_type=jnp.float32
        )

    def query_terms(dscore_block, key_block):
        return jnp.einsum(
            "hqk,khe->qhe", dscore_block, key_block, preferred_element_type=jnp.float32
        )

    held_keys = []
    held_values = []
    needs = []
    key_block, value_block = (key_heads, value_heads)
    scores = []
    for offset in range(SPAN_SH + 1):
        if offset > 0:
            key_block, value_block = shifted((key_block, value_block), "seq", 1)
        pair_mask = allowed_pairs(
            doc_ids, shard_index, shard_index - offset, row_count, shard_total
        )
        needed = jnp.any(pair_mask)
        held_keys.append(key_block)
        held_values.append(value_block)
        needs.append(needed)
        scores.append(guarded(score_block, (key_block, pair_mask)))
    row_peak = reduce(jnp.maximum, [jnp.max(block_scores, axis=2) for block_scores in scores])
    denominator = reduce(
        jnp.add,
        [jnp.sum(jnp.exp(block_scores - row_peak[..., None]), axis=2) for block_scores in scores],
    )
    weights = [
        (jnp.exp(block_scores - row_peak[..., None]) / denominator[..., None]).astype(jnp.bfloat16)
        for block_scores in scores
    ]
    attn_sum = reduce(
        jnp.add,
        [
            guarded(mix_block, (weights[offset], held_values[offset]))
            for offset in range(SPAN_SH + 1)
        ],
    )
    attn_out = attn_sum.astype(jnp.bfloat16).reshape(row_count, -1)
    dweights = [guarded(weight_grads, (held_values[offset],)) for offset in range(SPAN_SH + 1)]
    rowdot = reduce(
        jnp.add,
        [
            jnp.sum(weights[offset].astype(jnp.float32) * dweights[offset], axis=2)
            for offset in range(SPAN_SH + 1)
        ],
    )
    dscores = [
        (weights[offset].astype(jnp.float32) * (dweights[offset] - rowdot[..., None])).astype(
            jnp.bfloat16
        )
        for offset in range(SPAN_SH + 1)
    ]
    query_sum = reduce(
        jnp.add,
        [
            guarded(query_terms, (dscores[offset], held_keys[offset]))
            for offset in range(SPAN_SH + 1)
        ],
    )
    query_grad = (score_scale * query_sum).astype(jnp.bfloat16).reshape(row_count, -1)

    def key_terms(dscore_block, weight_block):
        key_part = score_scale * jnp.einsum(
            "hqk,qhe->khe", dscore_block, query_heads, preferred_element_type=jnp.float32
        )
        value_part = jnp.einsum(
            "hqk,qhe->khe", weight_block, cot_heads, preferred_element_type=jnp.float32
        )
        return (key_part, value_part)

    terms = [
        guarded(key_terms, (dscores[offset], weights[offset])) for offset in range(SPAN_SH + 1)
    ]
    grad_keys, grad_values = terms[SPAN_SH]
    for offset in range(SPAN_SH - 1, -1, -1):
        grad_keys, grad_values = shifted((grad_keys, grad_values), "seq", -1)
        grad_keys = grad_keys + terms[offset][0]
        grad_values = grad_values + terms[offset][1]
    key_grad = grad_keys.astype(jnp.bfloat16).reshape(row_count, -1)
    value_grad = grad_values.astype(jnp.bfloat16).reshape(row_count, -1)
    return (attn_out, query_grad, key_grad, value_grad)


def on_device(doc_ids, attn_queries, attn_keys, attn_values, attn_cot):
    shard_index = lax.axis_index("seq")
    attn_out, query_grad, key_grad, value_grad = attention_layer(
        doc_ids, shard_index, attn_queries, attn_keys, attn_values, attn_cot
    )
    return (attn_out, query_grad, key_grad, value_grad)


def solution(mesh):
    in_specs = (
        P(),
        P(("seq", "chan"), None),
        P(("seq", "chan"), None),
        P(("seq", "chan"), None),
        P(("seq", "chan"), None),
    )
    out_specs = (P("seq", "chan"), P("seq", "chan"), P("seq", "chan"), P("seq", "chan"))
    return jax.shard_map(
        on_device, mesh=mesh, in_specs=in_specs, out_specs=out_specs, check_vma=False
    )
```

profile of v0, /device:TPU:9, one launch (start us, length us, event | category | flops | bytes accessed | tf_op | source)
XLA Modules:
  0.0 405.9 jit_solution(16765148270065550172)
XLA Ops:
  3.0 4.8 %all-to-all-start = ((bf16[64,4,2048]{2,0,1:T(8,128)(2,1)}), bf16[64,4,2048]{2,0,1:T(8,128)(2,1)S(1)}, u32[]{:S(2)}, u32[]{:S(2)}) async-start(bf16[64,4,2048]{2,0,1:T(8,128)(2,1)} %bitcast.119), calls=%async_computation | async-start | bytes 2097152 | tf_op jit(solution)/shard_map/all_to_all | solution.py:38
  8.8 20.8 %all-to-all-done = bf16[64,4,2048]{2,0,1:T(8,128)(2,1)S(1)} async-done(((bf16[64,4,2048]{2,0,1:T(8,128)(2,1)}), bf16[64,4,2048]{2,0,1:T(8,128)(2,1)S(1)}, u32[]{:S(2)}, u32[]{:S(2)}) %all-to-all-start) | async-done | bytes 1048608 | tf_op jit(solution)/shard_map/all_to_all | solution.py:38
  29.6 6.9 %all-to-all-start.1 = ((bf16[64,4,2048]{2,0,1:T(8,128)(2,1)}), bf16[64,4,2048]{2,0,1:T(8,128)(2,1)S(1)}, u32[]{:S(2)}, u32[]{:S(2)}) async-start(bf16[64,4,2048]{2,0,1:T(8,128)(2,1)} %bitcast.120), calls=%async_computation.1 | async-start | bytes 2097152 | tf_op jit(solution)/shard_map/all_to_all | solution.py:39
  37.6 20.3 %all-to-all-done.1 = bf16[64,4,2048]{2,0,1:T(8,128)(2,1)S(1)} async-done(((bf16[64,4,2048]{2,0,1:T(8,128)(2,1)}), bf16[64,4,2048]{2,0,1:T(8,128)(2,1)S(1)}, u32[]{:S(2)}, u32[]{:S(2)}) %all-to-all-start.1) | async-done | bytes 1048608 | tf_op jit(solution)/shard_map/all_to_all | solution.py:39
  57.8 7.4 %all-to-all-start.2 = ((bf16[64,4,2048]{2,0,1:T(8,128)(2,1)}), bf16[64,4,2048]{2,0,1:T(8,128)(2,1)S(1)}, u32[]{:S(2)}, u32[]{:S(2)}) async-start(bf16[64,4,2048]{2,0,1:T(8,128)(2,1)} %bitcast.132), calls=%async_computation.2 | async-start | bytes 2097152 | tf_op jit(solution)/shard_map/all_to_all | solution.py:40
  67.5 19.0 %all-to-all-done.2 = bf16[64,4,2048]{2,0,1:T(8,128)(2,1)S(1)} async-done(((bf16[64,4,2048]{2,0,1:T(8,128)(2,1)}), bf16[64,4,2048]{2,0,1:T(8,128)(2,1)S(1)}, u32[]{:S(2)}, u32[]{:S(2)}) %all-to-all-start.2) | async-done | bytes 1048608 | tf_op jit(solution)/shard_map/all_to_all | solution.py:40
  87.5 7.4 %all-to-all-start.3 = ((bf16[64,4,2048]{2,0,1:T(8,128)(2,1)}), bf16[64,4,2048]{2,0,1:T(8,128)(2,1)S(1)}, u32[]{:S(2)}, u32[]{:S(2)}) async-start(bf16[64,4,2048]{2,0,1:T(8,128)(2,1)} %bitcast.118), calls=%async_computation.3 | async-start | bytes 2097152 | tf_op jit(solution)/shard_map/all_to_all | solution.py:41
  97.7 4.7 %collective-permute-start = (bf16[256,16,128]{2,0,1:T(8,128)(2,1)}, bf16[256,16,128]{2,0,1:T(8,128)(2,1)}, u32[]{:S(2)}, u32[]{:S(2)}) collective-permute-start(bf16[256,16,128]{2,0,1:T(8,128)(2,1)} %copy.71), channel_id=1, source_target_pairs={{0,4},{4,8},{8,12},{12,16},{16,20},{20,24},{24,28},{1,5},{5,9},{9,... | collective-permute-start | bytes 3145736 | tf_op jit(solution)/shard_map/ppermute | solution.py:18
  108.1 6.3 %collective-permute-done = bf16[256,16,128]{2,0,1:T(8,128)(2,1)} collective-permute-done((bf16[256,16,128]{2,0,1:T(8,128)(2,1)}, bf16[256,16,128]{2,0,1:T(8,128)(2,1)}, u32[]{:S(2)}, u32[]{:S(2)}) %collective-permute-start) | collective-permute-done | bytes 1048608 | tf_op jit(solution)/shard_map/ppermute | solution.py:18
  114.5 4.4 %collective-permute-start.1 = (bf16[256,16,128]{2,0,1:T(8,128)(2,1)}, bf16[256,16,128]{2,0,1:T(8,128)(2,1)}, u32[]{:S(2)}, u32[]{:S(2)}) collective-permute-start(bf16[256,16,128]{2,0,1:T(8,128)(2,1)} %collective-permute-done), channel_id=1, source_target_pairs={{0,4},{4,8},{8,12},{12,16},{16,20},{20,24},{24,28},{1,5},{5,9},{9,... | collective-permute-start | bytes 3145736 | tf_op jit(solution)/shard_map/ppermute | solution.py:18
  125.7 4.4 %collective-permute-start.5 = (bf16[256,16,128]{0,2,1:T(8,128)(2,1)}, bf16[256,16,128]{0,2,1:T(8,128)(2,1)S(1)}, u32[]{:S(2)}, u32[]{:S(2)}) collective-permute-start(bf16[256,16,128]{0,2,1:T(8,128)(2,1)} %collective-permute-done.4), channel_id=1, source_target_pairs={{0,4},{4,8},{8,12},{12,16},{16,20},{20,24},{24,28},{1,5},{5,9},{9,... | collective-permute-start | bytes 3145736 | tf_op jit(solution)/shard_map/ppermute | solution.py:18
  130.1 3.9 fusion.27
  136.9 4.4 %collective-permute-start.2 = (bf16[256,16,128]{2,0,1:T(8,128)(2,1)}, bf16[256,16,128]{2,0,1:T(8,128)(2,1)S(1)}, u32[]{:S(2)}, u32[]{:S(2)}) collective-permute-start(bf16[256,16,128]{2,0,1:T(8,128)(2,1)} %collective-permute-done.1), channel_id=1, source_target_pairs={{0,4},{4,8},{8,12},{12,16},{16,20},{20,24},{24,28},{1,5},{5,9},{9,... | collective-permute-start | bytes 3145736 | tf_op jit(solution)/shard_map/ppermute | solution.py:18
  143.4 4.8 %collective-permute-done.5 = bf16[256,16,128]{0,2,1:T(8,128)(2,1)S(1)} collective-permute-done((bf16[256,16,128]{0,2,1:T(8,128)(2,1)}, bf16[256,16,128]{0,2,1:T(8,128)(2,1)S(1)}, u32[]{:S(2)}, u32[]{:S(2)}) %collective-permute-start.5) | collective-permute-done | bytes 1048608 | tf_op jit(solution)/shard_map/ppermute | solution.py:18
  148.2 4.3 %collective-permute-start.6 = (bf16[256,16,128]{0,2,1:T(8,128)(2,1)S(1)}, bf16[256,16,128]{0,2,1:T(8,128)(2,1)S(1)}, u32[]{:S(2)}, u32[]{:S(2)}) collective-permute-start(bf16[256,16,128]{0,2,1:T(8,128)(2,1)S(1)} %collective-permute-done.5), channel_id=1, source_target_pairs={{0,4},{4,8},{8,12},{12,16},{16,20},{20,24},{24,28},{1,5},{5,9},{9,... | collective-permute-start | bytes 3145736 | tf_op jit(solution)/shard_map/ppermute | solution.py:18
  152.5 4.0 fusion.28
  159.4 4.3 %collective-permute-start.3 = (bf16[256,16,128]{2,0,1:T(8,128)(2,1)S(1)}, bf16[256,16,128]{2,0,1:T(8,128)(2,1)S(1)}, u32[]{:S(2)}, u32[]{:S(2)}) collective-permute-start(bf16[256,16,128]{2,0,1:T(8,128)(2,1)S(1)} %collective-permute-done.2), channel_id=1, source_target_pairs={{0,4},{4,8},{8,12},{12,16},{16,20},{20,24},{24,28},{1,5},{5,9},{9,... | collective-permute-start | bytes 3145736 | tf_op jit(solution)/shard_map/ppermute | solution.py:18
  166.4 4.1 %collective-permute-done.6 = bf16[256,16,128]{0,2,1:T(8,128)(2,1)S(1)} collective-permute-done((bf16[256,16,128]{0,2,1:T(8,128)(2,1)S(1)}, bf16[256,16,128]{0,2,1:T(8,128)(2,1)S(1)}, u32[]{:S(2)}, u32[]{:S(2)}) %collective-permute-start.6) | collective-permute-done | bytes 1048608 | tf_op jit(solution)/shard_map/ppermute | solution.py:18
  170.5 4.6 %collective-permute-start.7 = (bf16[256,16,128]{0,2,1:T(8,128)(2,1)S(1)}, bf16[256,16,128]{0,2,1:T(8,128)(2,1)}, u32[]{:S(2)}, u32[]{:S(2)}) collective-permute-start(bf16[256,16,128]{0,2,1:T(8,128)(2,1)S(1)} %collective-permute-done.6), channel_id=1, source_target_pairs={{0,4},{4,8},{8,12},{12,16},{16,20},{20,24},{24,28},{1,5},{5,9},{9,... | collective-permute-start | bytes 3145736 | tf_op jit(solution)/shard_map/ppermute | solution.py:18
  182.8 5.0 %fusion.16 = (f32[16,256]{1,0:T(8,128)S(1)}, f32[16,256]{1,0:T(8,128)S(1)}, f32[16,256]{1,0:T(8,128)S(1)}, f32[16,256]{1,0:T(8,128)S(1)}, f32[16,256]{1,0:T(8,128)S(1)}) fusion(f32[16,256,256]{1,2,0:T(8,128)S(1)} %get-tuple-element.59, f32[16,256]{1,0:T(8,128)S(1)} %maximum_maximum_fusion, pred[256,256]{0,1:T(8,128)(4,1)S(1)} %get-tuple-element.45, ...), kind=kLoop, calls=%fused_computation.41 | loop fusion | flops 20951040 | bytes 21397504 | tf_op jit(solution)/shard_map/reduce_sum | solution.py:94
  187.8 5.2 %collective-permute-done.7 = bf16[256,16,128]{0,2,1:T(8,128)(2,1)} collective-permute-done((bf16[256,16,128]{0,2,1:T(8,128)(2,1)S(1)}, bf16[256,16,128]{0,2,1:T(8,128)(2,1)}, u32[]{:S(2)}, u32[]{:S(2)}) %collective-permute-start.7) | collective-permute-done | bytes 1048608 | tf_op jit(solution)/shard_map/ppermute | solution.py:18
  193.0 19.9 %fusion.8 = (f32[16,256]{1,0:T(8,128)S(1)}, bf16[16,256,256]{1,2,0:T(8,128)(2,1)}, f32[16,256]{1,0:T(8,128)S(1)}, bf16[16,256,256]{1,2,0:T(8,128)(2,1)}, f32[16,...) fusion(f32[16,256]{1,0:T(8,128)S(1)} %add_add_fusion.1, ...), kind=kOutput, calls=%fused_computation.18 | convolution fusion | flops 310358016 | bytes 54968320 | tf_op jit(solution)/shard_map/qhe,khe->hqk/dot_general | solution.py:66
  213.0 3.8 convolution_bitcast_fusion
  218.7 13.2 %fusion.9 = (bf16[16,256,256]{1,2,0:T(8,128)(2,1)}, bf16[16,256,256]{1,2,0:T(8,128)(2,1)}, bf16[16,256,256]{1,2,0:T(8,128)(2,1)}, bf16[16,256,256]{1,2,0:T(8,128)(2,1)S(1)}, bf16[16,256,256]{1,2,0:T(8,128)(2,1)S(1)}) fusion(bf16[16,256,256]{1,2,0:T(8,128)(2,1)} %get-tuple-element.26, f32[16,256,256]{1,2,0:T(8,128)} %get-tuple-element.60, ...), kind=kLoop, calls=%fused_computation.19 | loop fusion | flops 20971520 | bytes 41959424 | tf_op jit(solution)/shard_map/convert_element_type | solution.py:117
  238.0 7.2 %collective-permute-done.12 = f32[256,16,128]{2,0,1:T(8,128)} collective-permute-done((f32[256,16,128]{2,0,1:T(8,128)}, f32[256,16,128]{2,0,1:T(8,128)}, u32[]{:S(2)}, u32[]{:S(2)}) %collective-permute-start.12) | collective-permute-done | bytes 2097184 | tf_op jit(solution)/shard_map/ppermute | solution.py:18
  249.5 18.1 %collective-permute-done.8 = f32[256,16,128]{0,2,1:T(8,128)S(1)} collective-permute-done((f32[256,16,128]{0,2,1:T(8,128)S(1)}, f32[256,16,128]{0,2,1:T(8,128)S(1)}, u32[]{:S(2)}, u32[]{:S(2)}) %collective-permute-start.8) | collective-permute-done | bytes 2097184 | tf_op jit(solution)/shard_map/ppermute | solution.py:18
  277.2 12.9 %collective-permute-done.13 = f32[256,16,128]{2,0,1:T(8,128)S(1)} collective-permute-done((f32[256,16,128]{2,0,1:T(8,128)S(1)}, f32[256,16,128]{2,0,1:T(8,128)S(1)}, u32[]{:S(2)}, u32[]{:S(2)}) %collective-permute-start.13) | collective-permute-done | bytes 2097184 | tf_op jit(solution)/shard_map/ppermute | solution.py:18
  292.3 20.2 %collective-permute-done.9 = f32[256,16,128]{0,2,1:T(8,128)S(1)} collective-permute-done((f32[256,16,128]{0,2,1:T(8,128)S(1)}, f32[256,16,128]{0,2,1:T(8,128)S(1)}, u32[]{:S(2)}, u32[]{:S(2)}) %collective-permute-start.9) | collective-permute-done | bytes 2097184 | tf_op jit(solution)/shard_map/ppermute | solution.py:18
  323.1 11.9 %collective-permute-done.14 = f32[256,16,128]{2,0,1:T(8,128)S(1)} collective-permute-done((f32[256,16,128]{2,0,1:T(8,128)S(1)}, f32[256,16,128]{2,0,1:T(8,128)S(1)}, u32[]{:S(2)}, u32[]{:S(2)}) %collective-permute-start.14) | collective-permute-done | bytes 2097184 | tf_op jit(solution)/shard_map/ppermute | solution.py:18
  338.7 18.8 %collective-permute-done.10 = f32[256,16,128]{0,2,1:T(8,128)S(1)} collective-permute-done((f32[256,16,128]{0,2,1:T(8,128)S(1)}, f32[256,16,128]{0,2,1:T(8,128)S(1)}, u32[]{:S(2)}, u32[]{:S(2)}) %collective-permute-start.10) | collective-permute-done | bytes 2097184 | tf_op jit(solution)/shard_map/ppermute | solution.py:18
  372.5 3.8 fusion.36
  385.5 17.0 %collective-permute-done.11 = f32[256,16,128]{0,2,1:T(8,128)} collective-permute-done((f32[256,16,128]{0,2,1:T(8,128)}, f32[256,16,128]{0,2,1:T(8,128)}, u32[]{:S(2)}, u32[]{:S(2)}) %collective-permute-start.11) | collective-permute-done | bytes 2097184 | tf_op jit(solution)/shard_map/ppermute | solution.py:18
  (134 shorter events, 107.0 us)
Async XLA Ops:
  3.0 26.6 %all-to-all-start = ((bf16[64,4,2048]{2,0,1:T(8,128)(2,1)}), bf16[64,4,2048]{2,0,1:T(8,128)(2,1)S(1)}, u32[]{:S(2)}, u32[]{:S(2)}) async-start(bf16[64,4,2048]{2,0,1:T(8,128)(2,1)} %bitcast.119), calls=%async_computation | async-start | bytes 2097152 | tf_op jit(solution)/shard_map/all_to_all | solution.py:38
  8.8 27.7 %copy-start.28 = (bf16[64,8192]{1,0:T(8,128)(2,1)S(1)}, bf16[64,8192]{1,0:T(8,128)(2,1)}, u32[]{:S(2)}) copy-start(bf16[64,8192]{1,0:T(8,128)(2,1)} %param.8) | copy-start | bytes 3145732
  29.6 28.2 %all-to-all-start.1 = ((bf16[64,4,2048]{2,0,1:T(8,128)(2,1)}), bf16[64,4,2048]{2,0,1:T(8,128)(2,1)S(1)}, u32[]{:S(2)}, u32[]{:S(2)}) async-start(bf16[64,4,2048]{2,0,1:T(8,128)(2,1)} %bitcast.120), calls=%async_computation.1 | async-start | bytes 2097152 | tf_op jit(solution)/shard_map/all_to_all | solution.py:39
  57.8 9.7 %copy-start.24 = (bf16[64,4,2048]{2,0,1:T(8,128)(2,1)}, bf16[64,4,2048]{2,0,1:T(8,128)(2,1)S(1)}, u32[]{:S(2)}) copy-start(bf16[64,4,2048]{2,0,1:T(8,128)(2,1)S(1)} %all-to-all-done.1) | copy-start | bytes 3145732
  57.8 28.7 %all-to-all-start.2 = ((bf16[64,4,2048]{2,0,1:T(8,128)(2,1)}), bf16[64,4,2048]{2,0,1:T(8,128)(2,1)S(1)}, u32[]{:S(2)}, u32[]{:S(2)}) async-start(bf16[64,4,2048]{2,0,1:T(8,128)(2,1)} %bitcast.132), calls=%async_computation.2 | async-start | bytes 2097152 | tf_op jit(solution)/shard_map/all_to_all | solution.py:40
  87.5 34.8 %all-to-all-start.3 = ((bf16[64,4,2048]{2,0,1:T(8,128)(2,1)}), bf16[64,4,2048]{2,0,1:T(8,128)(2,1)S(1)}, u32[]{:S(2)}, u32[]{:S(2)}) async-start(bf16[64,4,2048]{2,0,1:T(8,128)(2,1)} %bitcast.118), calls=%async_computation.3 | async-start | bytes 2097152 | tf_op jit(solution)/shard_map/all_to_all | solution.py:41
  94.9 7.5 %copy-start.26 = (bf16[64,4,2048]{2,0,1:T(8,128)(2,1)S(1)}, bf16[64,4,2048]{2,0,1:T(8,128)(2,1)}, u32[]{:S(2)}) copy-start(bf16[64,4,2048]{2,0,1:T(8,128)(2,1)} %copy-done.25) | copy-start | bytes 3145732
  97.7 16.8 %collective-permute-start = (bf16[256,16,128]{2,0,1:T(8,128)(2,1)}, bf16[256,16,128]{2,0,1:T(8,128)(2,1)}, u32[]{:S(2)}, u32[]{:S(2)}) collective-permute-start(bf16[256,16,128]{2,0,1:T(8,128)(2,1)} %copy.71), channel_id=1, source_target_pairs={{0,4},{4,8},{8,12},{12,16},{16,20},{20,24},{24,28},{1,5},{5,9},{9,... | collective-permute-start | bytes 3145736 | tf_op jit(solution)/shard_map/ppermute | solution.py:18
  106.1 19.6 %collective-permute-start.4 = (bf16[256,16,128]{0,2,1:T(8,128)(2,1)}, bf16[256,16,128]{0,2,1:T(8,128)(2,1)}, u32[]{:S(2)}, u32[]{:S(2)}) collective-permute-start(bf16[256,16,128]{0,2,1:T(8,128)(2,1)} %copy.53), channel_id=1, source_target_pairs={{0,4},{4,8},{8,12},{12,16},{16,20},{20,24},{24,28},{1,5},{5,9},{9,... | collective-permute-start | bytes 3145736 | tf_op jit(solution)/shard_map/ppermute | solution.py:18
  114.5 22.5 %collective-permute-start.1 = (bf16[256,16,128]{2,0,1:T(8,128)(2,1)}, bf16[256,16,128]{2,0,1:T(8,128)(2,1)}, u32[]{:S(2)}, u32[]{:S(2)}) collective-permute-start(bf16[256,16,128]{2,0,1:T(8,128)(2,1)} %collective-permute-done), channel_id=1, source_target_pairs={{0,4},{4,8},{8,12},{12,16},{16,20},{20,24},{24,28},{1,5},{5,9},{9,... | collective-permute-start | bytes 3145736 | tf_op jit(solution)/shard_map/ppermute | solution.py:18
  125.7 22.5 %collective-permute-start.5 = (bf16[256,16,128]{0,2,1:T(8,128)(2,1)}, bf16[256,16,128]{0,2,1:T(8,128)(2,1)S(1)}, u32[]{:S(2)}, u32[]{:S(2)}) collective-permute-start(bf16[256,16,128]{0,2,1:T(8,128)(2,1)} %collective-permute-done.4), channel_id=1, source_target_pairs={{0,4},{4,8},{8,12},{12,16},{16,20},{20,24},{24,28},{1,5},{5,9},{9,... | collective-permute-start | bytes 3145736 | tf_op jit(solution)/shard_map/ppermute | solution.py:18
  134.9 47.9 %copy-start.10 = (f32[16,256,256]{1,2,0:T(8,128)}, f32[16,256,256]{1,2,0:T(8,128)S(1)}, u32[]{:S(2)}) copy-start(f32[16,256,256]{1,2,0:T(8,128)S(1)} %get-tuple-element.57) | copy-start | bytes 12582916
  136.9 22.5 %collective-permute-start.2 = (bf16[256,16,128]{2,0,1:T(8,128)(2,1)}, bf16[256,16,128]{2,0,1:T(8,128)(2,1)S(1)}, u32[]{:S(2)}, u32[]{:S(2)}) collective-permute-start(bf16[256,16,128]{2,0,1:T(8,128)(2,1)} %collective-permute-done.1), channel_id=1, source_target_pairs={{0,4},{4,8},{8,12},{12,16},{16,20},{20,24},{24,28},{1,5},{5,9},{9,... | collective-permute-start | bytes 3145736 | tf_op jit(solution)/shard_map/ppermute | solution.py:18
  143.4 39.4 %copy-start.11 = (f32[16,256,256]{1,2,0:T(8,128)}, f32[16,256,256]{1,2,0:T(8,128)S(1)}, u32[]{:S(2)}) copy-start(f32[16,256,256]{1,2,0:T(8,128)S(1)} %get-tuple-element.59) | copy-start | bytes 12582916
  148.2 15.5 %copy-start.21 = (bf16[256,16,128]{0,2,1:T(8,128)(2,1)}, bf16[256,16,128]{0,2,1:T(8,128)(2,1)S(1)}, u32[]{:S(2)}) copy-start(bf16[256,16,128]{0,2,1:T(8,128)(2,1)S(1)} %collective-permute-done.5) | copy-start | bytes 3145732
  148.2 22.4 %collective-permute-start.6 = (bf16[256,16,128]{0,2,1:T(8,128)(2,1)S(1)}, bf16[256,16,128]{0,2,1:T(8,128)(2,1)S(1)}, u32[]{:S(2)}, u32[]{:S(2)}) collective-permute-start(bf16[256,16,128]{0,2,1:T(8,128)(2,1)S(1)} %collective-permute-done.5), channel_id=1, source_target_pairs={{0,4},{4,8},{8,12},{12,16},{16,20},{20,24},{24,28},{1,5},{5,9},{9,... | collective-permute-start | bytes 3145736 | tf_op jit(solution)/shard_map/ppermute | solution.py:18
  158.5 24.3 %copy-start.12 = (f32[16,256,256]{1,2,0:T(8,128)}, f32[16,256,256]{1,2,0:T(8,128)S(1)}, u32[]{:S(2)}) copy-start(f32[16,256,256]{1,2,0:T(8,128)S(1)} %get-tuple-element.55) | copy-start | bytes 12582916
  159.4 18.4 %copy-start.17 = (bf16[256,16,128]{2,0,1:T(8,128)(2,1)}, bf16[256,16,128]{2,0,1:T(8,128)(2,1)S(1)}, u32[]{:S(2)}) copy-start(bf16[256,16,128]{2,0,1:T(8,128)(2,1)S(1)} %collective-permute-done.2) | copy-start | bytes 3145732
  159.4 22.4 %collective-permute-start.3 = (bf16[256,16,128]{2,0,1:T(8,128)(2,1)S(1)}, bf16[256,16,128]{2,0,1:T(8,128)(2,1)S(1)}, u32[]{:S(2)}, u32[]{:S(2)}) collective-permute-start(bf16[256,16,128]{2,0,1:T(8,128)(2,1)S(1)} %collective-permute-done.2), channel_id=1, source_target_pairs={{0,4},{4,8},{8,12},{12,16},{16,20},{20,24},{24,28},{1,5},{5,9},{9,... | collective-permute-start | bytes 3145736 | tf_op jit(solution)/shard_map/ppermute | solution.py:18
  170.5 7.3 %copy-start.23 = (bf16[256,16,128]{0,2,1:T(8,128)(2,1)}, bf16[256,16,128]{0,2,1:T(8,128)(2,1)S(1)}, u32[]{:S(2)}) copy-start(bf16[256,16,128]{0,2,1:T(8,128)(2,1)S(1)} %collective-permute-done.6) | copy-start | bytes 3145732
  170.5 22.5 %collective-permute-start.7 = (bf16[256,16,128]{0,2,1:T(8,128)(2,1)S(1)}, bf16[256,16,128]{0,2,1:T(8,128)(2,1)}, u32[]{:S(2)}, u32[]{:S(2)}) collective-permute-start(bf16[256,16,128]{0,2,1:T(8,128)(2,1)S(1)} %collective-permute-done.6), channel_id=1, source_target_pairs={{0,4},{4,8},{8,12},{12,16},{16,20},{20,24},{24,28},{1,5},{5,9},{9,... | collective-permute-start | bytes 3145736 | tf_op jit(solution)/shard_map/ppermute | solution.py:18
  216.7 28.5 %collective-permute-start.12 = (f32[256,16,128]{2,0,1:T(8,128)}, f32[256,16,128]{2,0,1:T(8,128)}, u32[]{:S(2)}, u32[]{:S(2)}) collective-permute-start(f32[256,16,128]{2,0,1:T(8,128)} %convolution_bitcast_fusion), channel_id=1, source_target_pairs={{4,0},{8,4},{12,8},{16,12},{20,16},{24,20},{28,24},{5,1},{9,5},{13... | collective-permute-start | bytes 6291464 | tf_op jit(solution)/shard_map/ppermute | solution.py:18
  231.9 44.7 %copy-start.4 = (bf16[16,256,256]{1,2,0:T(8,128)(2,1)}, bf16[16,256,256]{1,2,0:T(8,128)(2,1)S(1)}, u32[]{:S(2)}) copy-start(bf16[16,256,256]{1,2,0:T(8,128)(2,1)S(1)} %get-tuple-element.39) | copy-start | bytes 6291460
  235.2 32.5 %collective-permute-start.8 = (f32[256,16,128]{0,2,1:T(8,128)S(1)}, f32[256,16,128]{0,2,1:T(8,128)S(1)}, u32[]{:S(2)}, u32[]{:S(2)}) collective-permute-start(f32[256,16,128]{0,2,1:T(8,128)S(1)} %multiply_bitcast_fusion), channel_id=1, source_target_pairs={{4,0},{8,4},{12,8},{16,12},{20,16},{24,20},{28,24},{5,1},{9,5},{13... | collective-permute-start | bytes 6291464 | tf_op jit(solution)/shard_map/ppermute | solution.py:18
  247.6 42.5 %collective-permute-start.13 = (f32[256,16,128]{2,0,1:T(8,128)S(1)}, f32[256,16,128]{2,0,1:T(8,128)S(1)}, u32[]{:S(2)}, u32[]{:S(2)}) collective-permute-start(f32[256,16,128]{2,0,1:T(8,128)S(1)} %bitcast_add_fusion.3), channel_id=1, source_target_pairs={{4,0},{8,4},{12,8},{16,12},{20,16},{24,20},{28,24},{5,1},{9,5},{13... | collective-permute-start | bytes 6291464 | tf_op jit(solution)/shard_map/ppermute | solution.py:18
  268.5 44.1 %collective-permute-start.9 = (f32[256,16,128]{0,2,1:T(8,128)S(1)}, f32[256,16,128]{0,2,1:T(8,128)S(1)}, u32[]{:S(2)}, u32[]{:S(2)}) collective-permute-start(f32[256,16,128]{0,2,1:T(8,128)S(1)} %bitcast_add_fusion.7), channel_id=1, source_target_pairs={{4,0},{8,4},{12,8},{16,12},{20,16},{24,20},{28,24},{5,1},{9,5},{13... | collective-permute-start | bytes 6291464 | tf_op jit(solution)/shard_map/ppermute | solution.py:18
  290.4 44.6 %collective-permute-start.14 = (f32[256,16,128]{2,0,1:T(8,128)S(1)}, f32[256,16,128]{2,0,1:T(8,128)S(1)}, u32[]{:S(2)}, u32[]{:S(2)}) collective-permute-start(f32[256,16,128]{2,0,1:T(8,128)S(1)} %bitcast_add_fusion.2), channel_id=1, source_target_pairs={{4,0},{8,4},{12,8},{16,12},{20,16},{24,20},{28,24},{5,1},{9,5},{13... | collective-permute-start | bytes 6291464 | tf_op jit(solution)/shard_map/ppermute | solution.py:18
  312.9 44.6 %collective-permute-start.10 = (f32[256,16,128]{0,2,1:T(8,128)S(1)}, f32[256,16,128]{0,2,1:T(8,128)S(1)}, u32[]{:S(2)}, u32[]{:S(2)}) collective-permute-start(f32[256,16,128]{0,2,1:T(8,128)S(1)} %bitcast_add_fusion.6), channel_id=1, source_target_pairs={{4,0},{8,4},{12,8},{16,12},{20,16},{24,20},{28,24},{5,1},{9,5},{13... | collective-permute-start | bytes 6291464 | tf_op jit(solution)/shard_map/ppermute | solution.py:18
  336.6 24.7 %copy-start.22 = (bf16[256,16,128]{0,2,1:T(8,128)(2,1)S(1)}, bf16[256,16,128]{0,2,1:T(8,128)(2,1)}, u32[]{:S(2)}) copy-start(bf16[256,16,128]{0,2,1:T(8,128)(2,1)} %copy-done.21) | copy-start | bytes 3145732
  336.6 43.4 %collective-permute-start.15 = (f32[256,16,128]{2,0,1:T(8,128)}, f32[256,16,128]{2,0,1:T(8,128)}, u32[]{:S(2)}, u32[]{:S(2)}) collective-permute-start(f32[256,16,128]{2,0,1:T(8,128)} %bitcast_add_fusion.1), channel_id=1, source_target_pairs={{4,0},{8,4},{12,8},{16,12},{20,16},{24,20},{28,24},{5,1},{9,5},{13... | collective-permute-start | bytes 6291464 | tf_op jit(solution)/shard_map/ppermute | solution.py:18
  359.2 43.4 %collective-permute-start.11 = (f32[256,16,128]{0,2,1:T(8,128)}, f32[256,16,128]{0,2,1:T(8,128)}, u32[]{:S(2)}, u32[]{:S(2)}) collective-permute-start(f32[256,16,128]{0,2,1:T(8,128)} %bitcast_add_fusion.5), channel_id=1, source_target_pairs={{4,0},{8,4},{12,8},{16,12},{20,16},{24,20},{28,24},{5,1},{9,5},{13... | collective-permute-start | bytes 6291464 | tf_op jit(solution)/shard_map/ppermute | solution.py:18
  381.9 20.6 %copy-start.15 = (f32[16,256,128]{1,2,0:T(8,128)S(1)}, f32[16,256,128]{1,2,0:T(8,128)}, u32[]{:S(2)}) copy-start(f32[16,256,128]{1,2,0:T(8,128)} %fusion.36) | copy-start | bytes 6291460
  (20 other events, 77.4 us)
where the time goes:
time: 408 us; the launch traced here: 406 us
  waiting for transfers between devices  196 us (48%)
  matrix products  77.3 us (19%)
  starting transfers between devices  75.3 us (18%)
  local copies, waits for them, and re-layouts  29.3 us (7%)
  other arithmetic  26.6 us (7%)
    ppermute x16, waiting for transfers between devices, shifted(): return lax.ppermute(value, axis, pairs)  136 us
    ppermute x16, starting transfers between devices, shifted(): return lax.ppermute(value, axis, pairs)  48.8 us
    dot_general x5, matrix products, weight_grads(): jnp.einsum('qhe,khe->hqk', cot_heads, value_block, preferred_element_type...  33.3 us
    all_to_all x1, waiting for transfers between devices, attention_layer(): lax.all_to_all(attn_queries, 'chan', split_axis=1, concat_axis=0, tiled=T...  20.8 us
    all_to_all x1, waiting for transfers between devices, attention_layer(): lax.all_to_all(attn_keys, 'chan', split_axis=1, concat_axis=0, tiled=True)  20.3 us
    all_to_all x1, waiting for transfers between devices, attention_layer(): lax.all_to_all(attn_values, 'chan', split_axis=1, concat_axis=0, tiled=True)  19 us
    unnamed x72, local copies, waits for them, and re-layouts  14.3 us
    dot_general x5, matrix products, mix_block(): jnp.einsum('hqk,khe->qhe', weight_block, value_block, preferred_element_t...  13.8 us
  transfers between devices with their start and end apart: 20, of which 19 were waited for; matrix products, arithmetic and copies ran while one was open for 25% of the time, Pallas kernels for 0%

commit v1 on v0

v1 whole, which is shorter than its diff:
```python
import functools
import math

import jax
import jax.numpy as jnp
from jax import lax
from jax.experimental import pallas as pl
from jax.experimental.pallas import tpu as pltpu
from jax.sharding import PartitionSpec as P

HEAD_DIM = 128
DOC_MAX = 1024
NEG = -1e30
SCALE = HEAD_DIM ** (-0.5)
EXP_SCALE = SCALE * math.log2(math.e)


def dot_nt(a, b):
    return lax.dot_general(a, b, (((1,), (1,)), ((), ())), preferred_element_type=jnp.float32)


def dot_nn(a, b):
    return lax.dot_general(a, b, (((1,), (0,)), ((), ())), preferred_element_type=jnp.float32)


def dot_tn(a, b):
    return lax.dot_general(a, b, (((0,), (0,)), ((), ())), preferred_element_type=jnp.float32)


def attention_kernel(spans, count_ref, start_ref, in_ref, out_ref, key_acc, value_acc):
    rows = in_ref.shape[2]
    blocks, _, block, _ = out_ref.shape
    group = block // rows
    key_acc[...] = jnp.zeros_like(key_acc)
    value_acc[...] = jnp.zeros_like(value_acc)

    def tokens(which, first, count):
        return in_ref[pl.ds(first * group, count * group), which].reshape(count * block, HEAD_DIM)

    def work(i, span):
        low = i - (span - 1)
        width = span * block
        query = tokens(0, i, 1)
        cot = tokens(3, i, 1)
        key = tokens(1, low, span)
        value = tokens(2, low, span)
        start = start_ref[pl.ds(i * block, block), :] - low * block
        col = lax.broadcasted_iota(jnp.int32, (block, width), 1)
        row = lax.broadcasted_iota(jnp.int32, (block, width), 0) + (span - 1) * block
        allowed = (col >= start) & (col <= row)
        score = jnp.where(allowed, dot_nt(query, key), NEG)
        peak = jnp.max(score, axis=1, keepdims=True)
        expo = jnp.exp2((score - peak) * EXP_SCALE)
        inverse = 1.0 / jnp.sum(expo, axis=1, keepdims=True)
        weight = expo * inverse
        weight_low = weight.astype(jnp.bfloat16)
        mixed = dot_nn(weight_low, value)
        rowdot = jnp.sum(mixed * cot.astype(jnp.float32), axis=1, keepdims=True)
        dscore = (weight * (dot_nt(cot, value) - rowdot)).astype(jnp.bfloat16)
        out_ref[i, 0] = mixed.astype(jnp.bfloat16)
        out_ref[i, 1] = (SCALE * dot_nn(dscore, key)).astype(jnp.bfloat16)
        held = pl.ds(pl.multiple_of(low * block, block), width)
        key_acc[held, :] += dot_tn(dscore, query)
        value_acc[held, :] += dot_tn(weight_low, cot)

    def step(i, carry):
        for span in range(1, spans + 1):
            pl.when(count_ref[i] == span)(functools.partial(work, i, span))
        return carry

    lax.fori_loop(0, blocks, step, 0)

    def finish(i, carry):
        held = pl.ds(pl.multiple_of(i * block, block), block)
        out_ref[i, 2] = (SCALE * key_acc[held, :]).astype(jnp.bfloat16)
        out_ref[i, 3] = value_acc[held, :].astype(jnp.bfloat16)
        return carry

    lax.fori_loop(0, blocks, finish, 0)


def attention(count, start, packed, shards):
    sources, _, rows, _ = packed.shape
    total = sources * rows
    block = total // shards
    spans = min(shards, (DOC_MAX + block - 2) // block + 1)
    pairs = total * block * min(spans, 3)
    return pl.pallas_call(
        functools.partial(attention_kernel, spans),
        out_shape=jax.ShapeDtypeStruct((shards, 4, block, HEAD_DIM), jnp.bfloat16),
        in_specs=[
            pl.BlockSpec(memory_space=pltpu.SMEM),
            pl.BlockSpec(memory_space=pltpu.VMEM),
            pl.BlockSpec(memory_space=pltpu.VMEM),
        ],
        out_specs=pl.BlockSpec(memory_space=pltpu.VMEM),
        scratch_shapes=[
            pltpu.VMEM((total, HEAD_DIM), jnp.float32),
            pltpu.VMEM((total, HEAD_DIM), jnp.float32),
        ],
        compiler_params=pltpu.CompilerParams(vmem_limit_bytes=48 * 1024 * 1024),
        cost_estimate=pl.CostEstimate(
            flops=12 * HEAD_DIM * pairs, bytes_accessed=16 * total * HEAD_DIM, transcendentals=pairs
        ),
    )(count, start, packed)


def on_device(doc_ids, *inputs):
    shards = lax.axis_size("seq")
    chans = lax.axis_size("chan")
    rows, width = inputs[0].shape
    heads = width // HEAD_DIM // chans
    turns = max(1, heads // shards)
    owners = heads // turns
    copies = shards // owners
    block = rows * chans
    start = jnp.sum((doc_ids[None, :] < doc_ids[:, None]).astype(jnp.int32), axis=1)
    count = jnp.arange(shards, dtype=jnp.int32) - start[::block] // block + 1
    start = start[:, None]

    split = [x.reshape(rows, chans, turns, owners, HEAD_DIM) for x in inputs]
    results = []
    for turn in range(turns):
        parts = jnp.stack([x[:, :, turn].transpose(2, 1, 0, 3) for x in split], axis=2)
        parts = jnp.repeat(parts, copies, axis=0) if copies > 1 else parts
        parts = parts.reshape(shards * chans, 4, rows, HEAD_DIM)
        packed = lax.all_to_all(parts, ("seq", "chan"), split_axis=0, concat_axis=0, tiled=True)
        done = attention(count, start, packed, shards)
        results.append(lax.all_to_all(done, "seq", split_axis=0, concat_axis=0, tiled=True)[::copies])
    outs = []
    for which in range(4):
        cols = jnp.stack([x[:, which] for x in results], axis=0)
        outs.append(cols.transpose(2, 0, 1, 3).reshape(block, heads * HEAD_DIM))
    return tuple(outs)


def solution(mesh):
    spread = P(("seq", "chan"), None)
    in_specs = (P(), spread, spread, spread, spread)
    out_specs = (P("seq", "chan"),) * 4
    return jax.shard_map(
        on_device, mesh=mesh, in_specs=in_specs, out_specs=out_specs, check_vma=False
    )
```

time: 408 us -> 191 us (0.47)
  the two profiles are of different devices: /device:TPU:9 before, /device:TPU:0 now
where the time goes in v1:
time: 191 us; the launch traced here: 190 us
  waiting for transfers between devices  118 us (62%)
  local copies, waits for them, and re-layouts  22.3 us (12%)
  Pallas kernels  22.3 us (12%)
  starting transfers between devices  20.1 us (11%)
  other arithmetic  6.82 us (4%)
    all_to_all x2, waiting for transfers between devices, on_device(): lax.all_to_all(parts, ('seq', 'chan'), split_axis=0, concat_axis=0, tiled...  78.2 us
    all_to_all x2, waiting for transfers between devices, on_device(): lax.all_to_all(done, 'seq', split_axis=0, concat_axis=0, tiled=True)  39.6 us
    pallas_call x2, Pallas kernels, attention(): pl.pallas_call(functools.partial(attention_kernel, spans), out_shape=jax....  22.3 us
    unnamed x34, local copies, waits for them, and re-layouts  13.5 us
    all_to_all x2, starting transfers between devices, on_device(): lax.all_to_all(parts, ('seq', 'chan'), split_axis=0, concat_axis=0, tiled...  11.6 us
    all_to_all x2, starting transfers between devices, on_device(): lax.all_to_all(done, 'seq', split_axis=0, concat_axis=0, tiled=True)  8.58 us
    another operation x2, local copies, waits for them, and re-layouts, on_device(): cols = jnp.stack([x[:, which] for x in results], axis=0)  3.99 us
  transfers between devices with their start and end apart: 4, of which 4 were waited for; matrix products, arithmetic and copies ran while one was open for 3% of the time, Pallas kernels for 12%

profile of v1, /device:TPU:0, one launch (start us, length us, event | category | flops | bytes accessed | tf_op | source)
XLA Modules:
  0.0 190.2 jit_solution(6525197089042699086)
XLA Ops:
  0.6 1.5 copy.99
  2.5 0.8 copy-done.5
  4.1 0.8 copy-done.6
  5.2 1.0 fusion.2
  6.8 1.0 fusion.3
  8.0 1.6 pad_maximum_fusion
  9.6 7.3 %all-to-all-start = ((bf16[32,4,64,128]{3,2,1,0:T(8,128)(2,1)}), bf16[32,4,64,128]{3,2,1,0:T(8,128)(2,1)S(1)}, u32[]{:S(2)}, u32[]{:S(2)}) async-start(bf16[32,4,64,128]{3,2,1,0:T(8,128)(2,1)} %pad_maximum_fusion), calls=%async_computation | async-start | bytes 4194304 | tf_op jit(solution)/shard_map/all_to_all | solution.py:127
  17.3 0.6 copy-done.1
  18.4 1.6 pad_maximum_fusion.1
  20.0 44.5 %all-to-all-done.in_ref = bf16[32,4,64,128]{3,2,1,0:T(8,128)(2,1)S(1)} async-done(((bf16[32,4,64,128]{3,2,1,0:T(8,128)(2,1)}), bf16[32,4,64,128]{3,2,1,0:T(8,128)(2,1)S(1)}, u32[]{:S(2)}, u32[]{:S(2)}) %all-to-all-start) | async-done | bytes 2097184 | tf_op jit(solution)/shard_map/all_to_all | solution.py:127
  64.4 4.3 %all-to-all-start.2 = ((bf16[32,4,64,128]{3,2,1,0:T(8,128)(2,1)}), bf16[32,4,64,128]{3,2,1,0:T(8,128)(2,1)}, u32[]{:S(2)}, u32[]{:S(2)}) async-start(bf16[32,4,64,128]{3,2,1,0:T(8,128)(2,1)} %pad_maximum_fusion.1), calls=%async_computation.2 | async-start | bytes 4194304 | tf_op jit(solution)/shard_map/all_to_all | solution.py:127
  68.7 1.8 convert_reduce_fusion
  70.6 0.4 copy.69.start_ref
  71.0 9.9 %shard_map.84 = bf16[8,4,256,128]{3,2,1,0:T(8,128)(2,1)S(1)} custom-call(s32[8]{0:T(128)S(1)} %subtract_add_fusion.count_ref, s32[2048,1]{1,0:T(8,128)S(1)} %copy.69.start_ref, bf16[32,4,64,128]{3,2,1,0:T(8,128)(2,1)S(1)} %all-to-all-done.in_ref), custom_call_target="tpu_custom_call" | custom-call | flops 2415919104 | bytes 4194304 | tf_op jit(solution)/shard_map/pallas_call | solution.py:88
  80.9 1.3 copy-done
  82.3 33.7 %all-to-all-done.2.in_ref = bf16[32,4,64,128]{3,2,1,0:T(8,128)(2,1)} async-done(((bf16[32,4,64,128]{3,2,1,0:T(8,128)(2,1)}), bf16[32,4,64,128]{3,2,1,0:T(8,128)(2,1)}, u32[]{:S(2)}, u32[]{:S(2)}) %all-to-all-start.2) | async-done | bytes 2097184 | tf_op jit(solution)/shard_map/all_to_all | solution.py:127
  116.0 4.2 %all-to-all-start.1 = ((bf16[8,4,256,128]{3,2,1,0:T(8,128)(2,1)}), bf16[8,4,256,128]{3,2,1,0:T(8,128)(2,1)S(1)}, u32[]{:S(2)}, u32[]{:S(2)}) async-start(bf16[8,4,256,128]{3,2,1,0:T(8,128)(2,1)} %copy-done), calls=%async_computation.1 | async-start | bytes 4194304 | tf_op jit(solution)/shard_map/all_to_all | solution.py:129
  120.2 12.3 %shard_map.85 = bf16[8,4,256,128]{3,2,1,0:T(8,128)(2,1)} custom-call(s32[8]{0:T(128)S(1)} %subtract_add_fusion.count_ref, s32[2048,1]{1,0:T(8,128)S(1)} %copy.69.start_ref, bf16[32,4,64,128]{3,2,1,0:T(8,128)(2,1)} %all-to-all-done.2.in_ref), custom_call_target="tpu_custom_call" | custom-call | flops 2415919104 | bytes 4194304 | tf_op jit(solution)/shard_map/pallas_call | solution.py:88
  132.5 14.3 %all-to-all-done.1 = bf16[8,4,256,128]{3,2,1,0:T(8,128)(2,1)S(1)} async-done(((bf16[8,4,256,128]{3,2,1,0:T(8,128)(2,1)}), bf16[8,4,256,128]{3,2,1,0:T(8,128)(2,1)S(1)}, u32[]{:S(2)}, u32[]{:S(2)}) %all-to-all-start.1) | async-done | bytes 2097184 | tf_op jit(solution)/shard_map/all_to_all | solution.py:129
  146.9 4.4 %all-to-all-start.3 = ((bf16[8,4,256,128]{3,2,1,0:T(8,128)(2,1)}), bf16[8,4,256,128]{3,2,1,0:T(8,128)(2,1)}, u32[]{:S(2)}, u32[]{:S(2)}) async-start(bf16[8,4,256,128]{3,2,1,0:T(8,128)(2,1)} %shard_map.85), calls=%async_computation.3 | async-start | bytes 4194304 | tf_op jit(solution)/shard_map/all_to_all | solution.py:129
  151.2 1.3 slice_bitcast_fusion.1
  152.6 25.3 %all-to-all-done.3 = bf16[8,4,256,128]{3,2,1,0:T(8,128)(2,1)} async-done(((bf16[8,4,256,128]{3,2,1,0:T(8,128)(2,1)}), bf16[8,4,256,128]{3,2,1,0:T(8,128)(2,1)}, u32[]{:S(2)}, u32[]{:S(2)}) %all-to-all-start.3) | async-done | bytes 2097184 | tf_op jit(solution)/shard_map/all_to_all | solution.py:129
  177.9 2.6 %slice_bitcast_fusion = (bf16[1,8,256,128]{3,2,1,0:T(8,128)(2,1)S(1)}, bf16[1,8,256,128]{3,2,1,0:T(8,128)(2,1)S(1)}, bf16[1,8,256,128]{3,2,1,0:T(8,128)(2,1)}, bf16[1,8,256,128]{3,2,1,0:T(8,128)(2,1)}) fusion(bf16[8,4,256,128]{3,2,1,0:T(8,128)(2,1)} %all-to-all-done.3), kind=kLoop, calls=%fused_computation.7 | loop fusion | bytes 4194304 | tf_op jit(solution)/shard_map/stack;squeeze | solution.py:132
  180.7 0.5 copy.80
  181.2 1.4 copy.85
  182.7 0.5 copy.82
  183.2 1.4 copy.86
  184.6 1.7 maximum_bitcast_fusion
  186.3 0.5 copy.76
  186.9 1.4 copy.83
  188.3 0.5 copy.78
  188.8 1.4 copy.84
  (30 shorter events, 3.3 us)
Async XLA Ops:
  2.1 1.2 copy-start.5
  3.6 1.2 copy-start.6
  5.1 1.4 copy-start.7
  9.6 54.8 %all-to-all-start = ((bf16[32,4,64,128]{3,2,1,0:T(8,128)(2,1)}), bf16[32,4,64,128]{3,2,1,0:T(8,128)(2,1)S(1)}, u32[]{:S(2)}, u32[]{:S(2)}) async-start(bf16[32,4,64,128]{3,2,1,0:T(8,128)(2,1)} %pad_maximum_fusion), calls=%async_computation | async-start | bytes 4194304 | tf_op jit(solution)/shard_map/all_to_all | solution.py:127
  16.9 1.0 copy-start.1
  16.9 1.2 copy-start.2
  20.0 48.7 %copy-start.8 = (s32[2048]{0:T(1024)S(1)}, s32[2048]{0:T(1024)}, u32[]{:S(2)}) copy-start(s32[2048]{0:T(1024)} %param.5) | copy-start | bytes 24580
  64.4 51.6 %all-to-all-start.2 = ((bf16[32,4,64,128]{3,2,1,0:T(8,128)(2,1)}), bf16[32,4,64,128]{3,2,1,0:T(8,128)(2,1)}, u32[]{:S(2)}, u32[]{:S(2)}) async-start(bf16[32,4,64,128]{3,2,1,0:T(8,128)(2,1)} %pad_maximum_fusion.1), calls=%async_computation.2 | async-start | bytes 4194304 | tf_op jit(solution)/shard_map/all_to_all | solution.py:127
  80.9 1.3 copy-start
  116.0 30.9 %all-to-all-start.1 = ((bf16[8,4,256,128]{3,2,1,0:T(8,128)(2,1)}), bf16[8,4,256,128]{3,2,1,0:T(8,128)(2,1)S(1)}, u32[]{:S(2)}, u32[]{:S(2)}) async-start(bf16[8,4,256,128]{3,2,1,0:T(8,128)(2,1)} %copy-done), calls=%async_computation.1 | async-start | bytes 4194304 | tf_op jit(solution)/shard_map/all_to_all | solution.py:129
  146.9 31.0 %all-to-all-start.3 = ((bf16[8,4,256,128]{3,2,1,0:T(8,128)(2,1)}), bf16[8,4,256,128]{3,2,1,0:T(8,128)(2,1)}, u32[]{:S(2)}, u32[]{:S(2)}) async-start(bf16[8,4,256,128]{3,2,1,0:T(8,128)(2,1)} %shard_map.85), calls=%async_computation.3 | async-start | bytes 4194304 | tf_op jit(solution)/shard_map/all_to_all | solution.py:129
  152.6 27.9 %copy-start.3 = (bf16[1,8,256,128]{3,2,1,0:T(8,128)(2,1)S(1)}, bf16[1,8,256,128]{3,2,1,0:T(8,128)(2,1)}, u32[]{:S(2)}) copy-start(bf16[1,8,256,128]{3,2,1,0:T(8,128)(2,1)} %get-tuple-element.16) | copy-start | bytes 1572868
  152.6 27.9 %copy-start.4 = (bf16[1,8,256,128]{3,2,1,0:T(8,128)(2,1)S(1)}, bf16[1,8,256,128]{3,2,1,0:T(8,128)(2,1)}, u32[]{:S(2)}) copy-start(bf16[1,8,256,128]{3,2,1,0:T(8,128)(2,1)} %get-tuple-element.17) | copy-start | bytes 1572868

commit v2 on v1

--- a/solution.py
+++ b/solution.py
@@ -27,7 +27,8 @@
     return lax.dot_general(a, b, (((0,), (0,)), ((), ())), preferred_element_type=jnp.float32)
 
 
-def attention_kernel(spans, count_ref, start_ref, in_ref, out_ref, key_acc, value_acc):
+def attention_kernel(spans, peers, count_ref, start_ref, target_ref, in_ref, *refs):
+    outs, (out_ref, key_acc, value_acc, sems) = refs[:peers], refs[peers:]
     rows = in_ref.shape[2]
     blocks, _, block, _ = out_ref.shape
     group = block // rows
@@ -77,32 +78,100 @@
         return carry
 
     lax.fori_loop(0, blocks, finish, 0)
-
-
-def attention(count, start, packed, shards):
+    moves = [
+        pltpu.make_async_copy(out_ref.at[target_ref[d]], outs[d], sems.at[d]) for d in range(peers)
+    ]
+    for move in moves:
+        move.start()
+    for move in moves:
+        move.wait()
+
+
+def attention(count, start, targets, packed):
     sources, _, rows, _ = packed.shape
+    shards = targets.shape[0]
     total = sources * rows
     block = total // shards
     spans = min(shards, (DOC_MAX + block - 2) // block + 1)
     pairs = total * block * min(spans, 3)
     return pl.pallas_call(
-        functools.partial(attention_kernel, spans),
-        out_shape=jax.ShapeDtypeStruct((shards, 4, block, HEAD_DIM), jnp.bfloat16),
+        functools.partial(attention_kernel, spans, shards),
+        out_shape=[jax.ShapeDtypeStruct((4, block, HEAD_DIM), jnp.bfloat16)] * shards,
         in_specs=[
             pl.BlockSpec(memory_space=pltpu.SMEM),
             pl.BlockSpec(memory_space=pltpu.VMEM),
+            pl.BlockSpec(memory_space=pltpu.SMEM),
             pl.BlockSpec(memory_space=pltpu.VMEM),
         ],
-        out_specs=pl.BlockSpec(memory_space=pltpu.VMEM),
+        out_specs=[pl.BlockSpec(memory_space=pl.ANY)] * shards,
         scratch_shapes=[
+            pltpu.VMEM((shards, 4, block, HEAD_DIM), jnp.bfloat16),
             pltpu.VMEM((total, HEAD_DIM), jnp.float32),
             pltpu.VMEM((total, HEAD_DIM), jnp.float32),
+            pltpu.SemaphoreType.DMA((shards,)),
         ],
         compiler_params=pltpu.CompilerParams(vmem_limit_bytes=48 * 1024 * 1024),
         cost_estimate=pl.CostEstimate(
             flops=12 * HEAD_DIM * pairs, bytes_accessed=16 * total * HEAD_DIM, transcendentals=pairs
         ),
-    )(count, start, packed)
+    )(count, start, targets, packed)
+
+
+def pack_kernel(owners, *refs):
+    ins, out_ref = refs[:4], refs[4]
+    for owner in range(owners):
+        for which in range(4):
+            out_ref[owner, 0, which] = ins[which][:, owner * HEAD_DIM : (owner + 1) * HEAD_DIM]
+
+
+def pack(inputs, chans, turns, turn):
+    rows, width = inputs[0].shape
+    owners = width // HEAD_DIM // chans // turns
+    shape = (owners, chans, 4, rows, HEAD_DIM)
+    return pl.pallas_call(
+        functools.partial(pack_kernel, owners),
+        grid=(chans,),
+        out_shape=jax.ShapeDtypeStruct(shape, jnp.bfloat16),
+        in_specs=[pl.BlockSpec((rows, owners * HEAD_DIM), lambda c: (0, c * turns + turn))] * 4,
+        out_specs=pl.BlockSpec((owners, 1, 4, rows, HEAD_DIM), lambda c: (0, c, 0, 0, 0)),
+        cost_estimate=pl.CostEstimate(
+            flops=0, bytes_accessed=4 * math.prod(shape), transcendentals=0
+        ),
+    )(*inputs)
+
+
+def unpack_kernel(count, column_ref, *refs):
+    blocks, outs, sems = refs[:count], refs[-5:-1], refs[-1]
+    moves = []
+    for b in range(count):
+        columns = pl.ds(pl.multiple_of(column_ref[b] * HEAD_DIM, HEAD_DIM), HEAD_DIM)
+        for which in range(4):
+            moves.append(
+                pltpu.make_async_copy(
+                    blocks[b].at[which], outs[which].at[:, columns], sems.at[b, which]
+                )
+            )
+    for move in moves:
+        move.start()
+    for move in moves:
+        move.wait()
+
+
+def unpack(blocks, columns, width, held):
+    count = len(blocks)
+    rows = blocks[0].shape[1]
+    anywhere = pl.BlockSpec(memory_space=pl.ANY)
+    return pl.pallas_call(
+        functools.partial(unpack_kernel, count),
+        out_shape=[jax.ShapeDtypeStruct((rows, width), jnp.bfloat16)] * 4,
+        in_specs=[pl.BlockSpec(memory_space=pltpu.SMEM)] + [anywhere] * (count + len(held)),
+        out_specs=[anywhere] * 4,
+        scratch_shapes=[pltpu.SemaphoreType.DMA((count, 4))],
+        input_output_aliases={1 + count + i: i for i in range(len(held))},
+        cost_estimate=pl.CostEstimate(
+            flops=0, bytes_accessed=16 * count * rows * HEAD_DIM, transcendentals=0
+        ),
+    )(columns, *blocks, *held)
 
 
 def on_device(doc_ids, *inputs):
@@ -117,20 +186,27 @@
     start = jnp.sum((doc_ids[None, :] < doc_ids[:, None]).astype(jnp.int32), axis=1)
     count = jnp.arange(shards, dtype=jnp.int32) - start[::block] // block + 1
     start = start[:, None]
-
-    split = [x.reshape(rows, chans, turns, owners, HEAD_DIM) for x in inputs]
-    results = []
+    peers = jnp.bitwise_xor(lax.axis_index("seq"), jnp.arange(shards, dtype=jnp.int32))
+
+    outs = ()
     for turn in range(turns):
-        parts = jnp.stack([x[:, :, turn].transpose(2, 1, 0, 3) for x in split], axis=2)
+        parts = pack(inputs, chans, turns, turn)
         parts = jnp.repeat(parts, copies, axis=0) if copies > 1 else parts
         parts = parts.reshape(shards * chans, 4, rows, HEAD_DIM)
         packed = lax.all_to_all(parts, ("seq", "chan"), split_axis=0, concat_axis=0, tiled=True)
-        done = attention(count, start, packed, shards)
-        results.append(lax.all_to_all(done, "seq", split_axis=0, concat_axis=0, tiled=True)[::copies])
-    outs = []
-    for which in range(4):
-        cols = jnp.stack([x[:, which] for x in results], axis=0)
-        outs.append(cols.transpose(2, 0, 1, 3).reshape(block, heads * HEAD_DIM))
+        blocks = attention(count, start, peers, packed)
+        if copies == 1:
+            blocks = [blocks[0]] + [
+                lax.ppermute(blocks[d], "seq", [(s, s ^ d) for s in range(shards)])
+                for d in range(1, shards)
+            ]
+            columns = peers
+        else:
+            order = jnp.stack(blocks)[peers]
+            order = lax.all_to_all(order, "seq", split_axis=0, concat_axis=0, tiled=True)
+            blocks = [order[owner * copies] for owner in range(owners)]
+            columns = jnp.arange(owners, dtype=jnp.int32)
+        outs = unpack(blocks, columns + turn * owners, heads * HEAD_DIM, outs)
     return tuple(outs)
 
 

time: 191 us -> 281 us (1.47)
  the two profiles are of different devices: /device:TPU:0 before, /device:TPU:9 now
where the time goes in v2:
time: 281 us; the launch traced here: 280 us
  Pallas kernels  162 us (58%)
  waiting for transfers between devices  82.6 us (29%)
  starting transfers between devices  25 us (9%)
  local copies, waits for them, and re-layouts  7.15 us (3%)
    pallas_call x2, Pallas kernels, unpack(): pl.pallas_call(functools.partial(unpack_kernel, count), out_shape=[jax.Sh...  131 us
    all_to_all x2, waiting for transfers between devices, on_device(): lax.all_to_all(parts, ('seq', 'chan'), split_axis=0, concat_axis=0, tiled...  71.3 us
    pallas_call x2, Pallas kernels, attention(): pl.pallas_call(functools.partial(attention_kernel, spans, shards), out_sh...  22.4 us
    ppermute x14, starting transfers between devices, on_device(): lax.ppermute(blocks[d], 'seq', [(s, s ^ d) for s in range(shards)])  15.1 us
    ppermute x14, waiting for transfers between devices, on_device(): lax.ppermute(blocks[d], 'seq', [(s, s ^ d) for s in range(shards)])  11.3 us
    all_to_all x2, starting transfers between devices, on_device(): lax.all_to_all(parts, ('seq', 'chan'), split_axis=0, concat_axis=0, tiled...  9.86 us
    pallas_call x2, Pallas kernels, pack(): pl.pallas_call(functools.partial(pack_kernel, owners), grid=(chans,), out...  7.97 us
    unnamed x34, local copies, waits for them, and re-layouts  6.69 us
  transfers between devices with their start and end apart: 16, of which 5 were waited for; matrix products, arithmetic and copies ran while one was open for 1% of the time, Pallas kernels for 33%

profile of v2, /device:TPU:9, one launch (start us, length us, event | category | flops | bytes accessed | tf_op | source)
XLA Modules:
  0.0 279.7 jit_solution(11841780728366846279)
XLA Ops:
  0.6 4.0 %shard_map.86 = bf16[8,4,4,64,128]{4,3,2,1,0:T(8,128)(2,1)} custom-call(bf16[64,8192]{1,0:T(8,128)(2,1)} %refs_0_.3, bf16[64,8192]{1,0:T(8,128)(2,1)} %refs_1_.3, bf16[64,8192]{1,0:T(8,128)(2,1)} %refs_2_.3, bf16[64,8192]{1,0:T(8,128)(2,1)} %refs_3_.3), custom_call_target="tpu_custom_call" | custom-call | bytes 4194304 | tf_op jit(solution)/shard_map/pallas_call | solution.py:131
  4.6 6.4 %all-to-all-start.1 = ((bf16[32,4,64,128]{3,2,1,0:T(8,128)(2,1)}), bf16[32,4,64,128]{3,2,1,0:T(8,128)(2,1)S(1)}, u32[]{:S(2)}, u32[]{:S(2)}) async-start(bf16[32,4,64,128]{3,2,1,0:T(8,128)(2,1)} %bitcast.4), calls=%async_computation.1 | async-start | bytes 4194304 | tf_op jit(solution)/shard_map/all_to_all | solution.py:196
  11.0 4.0 %shard_map.84 = bf16[8,4,4,64,128]{4,3,2,1,0:T(8,128)(2,1)} custom-call(bf16[64,8192]{1,0:T(8,128)(2,1)} %refs_0_.3, bf16[64,8192]{1,0:T(8,128)(2,1)} %refs_1_.3, bf16[64,8192]{1,0:T(8,128)(2,1)} %refs_2_.3, bf16[64,8192]{1,0:T(8,128)(2,1)} %refs_3_.3), custom_call_target="tpu_custom_call" | custom-call | bytes 4194304 | tf_op jit(solution)/shard_map/pallas_call | solution.py:131
  15.0 44.2 %all-to-all-done.1.in_ref = bf16[32,4,64,128]{3,2,1,0:T(8,128)(2,1)S(1)} async-done(((bf16[32,4,64,128]{3,2,1,0:T(8,128)(2,1)}), bf16[32,4,64,128]{3,2,1,0:T(8,128)(2,1)S(1)}, u32[]{:S(2)}, u32[]{:S(2)}) %all-to-all-start.1) | async-done | bytes 2097184 | tf_op jit(solution)/shard_map/all_to_all | solution.py:196
  59.1 1.3 copy-done
  60.5 3.5 %all-to-all-start = ((bf16[32,4,64,128]{3,2,1,0:T(8,128)(2,1)}), bf16[32,4,64,128]{3,2,1,0:T(8,128)(2,1)S(1)}, u32[]{:S(2)}, u32[]{:S(2)}) async-start(bf16[32,4,64,128]{3,2,1,0:T(8,128)(2,1)} %bitcast.3), calls=%async_computation | async-start | bytes 4194304 | tf_op jit(solution)/shard_map/all_to_all | solution.py:196
  64.0 1.8 convert_reduce_fusion
  66.3 1.6 copy-done.1
  67.9 11.1 %shard_map.87 = (bf16[4,256,128]{2,1,0:T(8,128)(2,1)S(1)}, bf16[4,256,128]{2,1,0:T(8,128)(2,1)}, bf16[4,256,128]{2,1,0:T(8,128)(2,1)}, bf16[4,256,128]{2,1,0:T(8...) custom-call(s32[8]{0:T(128)S(1)} %get-tuple-element.44.count_ref, ...), custom_call_target="tpu_custom_call" | custom-call | flops 2415919104 | bytes 4194304 | tf_op jit(solution)/shard_map/pallas_call | solution.py:97
  79.0 0.7 copy-done.2
  79.7 0.7 copy-done.5
  80.4 0.7 copy-done.6
  81.5 1.2 collective-permute-start.8
  82.7 0.6 collective-permute-start.9
  83.3 1.2 collective-permute-start.10
  84.4 0.5 collective-permute-start.11
  85.0 27.2 %all-to-all-done.in_ref = bf16[32,4,64,128]{3,2,1,0:T(8,128)(2,1)S(1)} async-done(((bf16[32,4,64,128]{3,2,1,0:T(8,128)(2,1)}), bf16[32,4,64,128]{3,2,1,0:T(8,128)(2,1)S(1)}, u32[]{:S(2)}, u32[]{:S(2)}) %all-to-all-start) | async-done | bytes 2097184 | tf_op jit(solution)/shard_map/all_to_all | solution.py:196
  112.1 11.3 %shard_map.85 = (bf16[4,256,128]{2,1,0:T(8,128)(2,1)S(1)}, bf16[4,256,128]{2,1,0:T(8,128)(2,1)S(1)}, bf16[4,256,128]{2,1,0:T(8,128)(2,1)S(1)}, bf16[4,256,128]{2...) custom-call(s32[8]{0:T(128)S(1)} %get-tuple-element.44.count_ref, ...), custom_call_target="tpu_custom_call" | custom-call | flops 2415919104 | bytes 4194304 | tf_op jit(solution)/shard_map/pallas_call | solution.py:97
  123.4 0.7 copy-done.3
  124.1 1.4 collective-permute-start.12
  125.5 2.2 collective-permute-start.13
  127.8 2.0 collective-permute-start.2
  129.8 2.1 collective-permute-done.12.refs_6_
  132.0 1.7 collective-permute-start.3
  133.6 6.9 %collective-permute-done.13.refs_7_ = bf16[4,256,128]{2,1,0:T(8,128)(2,1)S(1)} collective-permute-done((bf16[4,256,128]{2,1,0:T(8,128)(2,1)}, bf16[4,256,128]{2,1,0:T(8,128)(2,1)S(1)}, u32[]{:S(2)}, u32[]{:S(2)}) %collective-permute-start.13) | collective-permute-done | bytes 262176 | tf_op jit(solution)/shard_map/ppermute | solution.py:200
  140.5 1.0 collective-permute-start.5
  141.5 2.3 collective-permute-done.1.refs_2_
  143.7 2.9 %collective-permute-start.6 = (bf16[4,256,128]{2,1,0:T(8,128)(2,1)S(1)}, bf16[4,256,128]{2,1,0:T(8,128)(2,1)S(1)}, u32[]{:S(2)}, u32[]{:S(2)}) collective-permute-start(bf16[4,256,128]{2,1,0:T(8,128)(2,1)S(1)} %get-tuple-element.31), channel_id=1, source_target_pairs={{0,28},{4,24},{8,20},{12,16},{16,12},{20,8},{24,4},{28,0},{1,29},{... | collective-permute-start | bytes 786440 | tf_op jit(solution)/shard_map/ppermute | solution.py:200
  146.7 0.6 broadcast_add_fusion.column_ref
  147.2 65.6 %shard_map.88 = (bf16[256,2048]{1,0:T(8,128)(2,1)}, bf16[256,2048]{1,0:T(8,128)(2,1)}, bf16[256,2048]{1,0:T(8,128)(2,1)}, bf16[256,2048]{1,0:T(8,128)(2,1)}) custom-call(s32[8]{0:T(128)} %copy-done.4, bf16[4,256,128]{2,1,0:T(8,128)(2,1)} %copy-done.2, bf16[4,256,128]{2,1,0:T(8,128)(2,1)} %collective-permute-done.7.refs_1_, ...), custom_call_target="tpu_custom_call" | custom-call | bytes 4194304 | tf_op jit(solution)/shard_map/pallas_call | solution.py:164
  213.0 0.6 copy-done.10
  213.9 65.6 %shard_map.89 = (bf16[256,2048]{1,0:T(8,128)(2,1)}, bf16[256,2048]{1,0:T(8,128)(2,1)}, bf16[256,2048]{1,0:T(8,128)(2,1)}, bf16[256,2048]{1,0:T(8,128)(2,1)}) custom-call(s32[8]{0:T(128)} %broadcast_add_fusion.column_ref, bf16[4,256,128]{2,1,0:T(8,128)(2,1)} %copy-done.3, ...), custom_call_target="tpu_custom_call", output_to_operand_aliasing={{0}: (9, {}), {1}: (10, {}), {2}: (11, {}), {3}: (12, {})} | custom-call | bytes 4194304 | tf_op jit(solution)/shard_map/pallas_call | solution.py:164
  (45 shorter events, 1.4 us)
Async XLA Ops:
  4.6 54.5 %all-to-all-start.1 = ((bf16[32,4,64,128]{3,2,1,0:T(8,128)(2,1)}), bf16[32,4,64,128]{3,2,1,0:T(8,128)(2,1)S(1)}, u32[]{:S(2)}, u32[]{:S(2)}) async-start(bf16[32,4,64,128]{3,2,1,0:T(8,128)(2,1)} %bitcast.4), calls=%async_computation.1 | async-start | bytes 4194304 | tf_op jit(solution)/shard_map/all_to_all | solution.py:196
  59.1 1.3 copy-start
  60.5 3.5 %copy-start.16 = (s32[2048]{0:T(1024)S(1)}, s32[2048]{0:T(1024)}, u32[]{:S(2)}) copy-start(s32[2048]{0:T(1024)} %param.5) | copy-start | bytes 24580
  60.5 51.7 %all-to-all-start = ((bf16[32,4,64,128]{3,2,1,0:T(8,128)(2,1)}), bf16[32,4,64,128]{3,2,1,0:T(8,128)(2,1)S(1)}, u32[]{:S(2)}, u32[]{:S(2)}) async-start(bf16[32,4,64,128]{3,2,1,0:T(8,128)(2,1)} %bitcast.3), calls=%async_computation | async-start | bytes 4194304 | tf_op jit(solution)/shard_map/all_to_all | solution.py:196
  66.3 45.9 %copy-start.4 = (s32[8]{0:T(128)}, s32[8]{0:T(128)S(1)}, u32[]{:S(2)}) copy-start(s32[8]{0:T(128)S(1)} %get-tuple-element.45.target_ref.column_ref) | copy-start | bytes 100
  66.3 1.6 copy-start.1
  79.0 0.7 copy-start.2
  79.7 0.7 copy-start.5
  80.4 0.7 copy-start.6
  81.1 43.0 %collective-permute-start.7 = (bf16[4,256,128]{2,1,0:T(8,128)(2,1)}, bf16[4,256,128]{2,1,0:T(8,128)(2,1)}, u32[]{:S(2)}, u32[]{:S(2)}) collective-permute-start(bf16[4,256,128]{2,1,0:T(8,128)(2,1)} %get-tuple-element.33), channel_id=1, source_target_pairs={{0,4},{4,0},{8,12},{12,8},{16,20},{20,16},{24,28},{28,24},{1,5},{5... | collective-permute-start | bytes 786440 | tf_op jit(solution)/shard_map/ppermute | solution.py:200
  81.5 44.0 %collective-permute-start.8 = (bf16[4,256,128]{2,1,0:T(8,128)(2,1)}, bf16[4,256,128]{2,1,0:T(8,128)(2,1)}, u32[]{:S(2)}, u32[]{:S(2)}) collective-permute-start(bf16[4,256,128]{2,1,0:T(8,128)(2,1)} %get-tuple-element.34), channel_id=1, source_target_pairs={{0,8},{4,12},{8,0},{12,4},{16,24},{20,28},{24,16},{28,20},{1,9},{5... | collective-permute-start | bytes 786440 | tf_op jit(solution)/shard_map/ppermute | solution.py:200
  82.7 45.0 %collective-permute-start.9 = (bf16[4,256,128]{2,1,0:T(8,128)(2,1)}, bf16[4,256,128]{2,1,0:T(8,128)(2,1)}, u32[]{:S(2)}, u32[]{:S(2)}) collective-permute-start(bf16[4,256,128]{2,1,0:T(8,128)(2,1)} %get-tuple-element.35), channel_id=1, source_target_pairs={{0,12},{4,8},{8,4},{12,0},{16,28},{20,24},{24,20},{28,16},{1,13},{... | collective-permute-start | bytes 786440 | tf_op jit(solution)/shard_map/ppermute | solution.py:200
  83.3 44.4 %collective-permute-start.10 = (bf16[4,256,128]{2,1,0:T(8,128)(2,1)}, bf16[4,256,128]{2,1,0:T(8,128)(2,1)}, u32[]{:S(2)}, u32[]{:S(2)}) collective-permute-start(bf16[4,256,128]{2,1,0:T(8,128)(2,1)} %get-tuple-element.36), channel_id=1, source_target_pairs={{0,16},{4,20},{8,24},{12,28},{16,0},{20,4},{24,8},{28,12},{1,17},{... | collective-permute-start | bytes 786440 | tf_op jit(solution)/shard_map/ppermute | solution.py:200
  84.4 43.4 %collective-permute-start.11 = (bf16[4,256,128]{2,1,0:T(8,128)(2,1)}, bf16[4,256,128]{2,1,0:T(8,128)(2,1)}, u32[]{:S(2)}, u32[]{:S(2)}) collective-permute-start(bf16[4,256,128]{2,1,0:T(8,128)(2,1)} %get-tuple-element.37), channel_id=1, source_target_pairs={{0,20},{4,16},{8,28},{12,24},{16,4},{20,0},{24,12},{28,8},{1,21},{... | collective-permute-start | bytes 786440 | tf_op jit(solution)/shard_map/ppermute | solution.py:200
  124.1 7.9 %collective-permute-start.12 = (bf16[4,256,128]{2,1,0:T(8,128)(2,1)}, bf16[4,256,128]{2,1,0:T(8,128)(2,1)S(1)}, u32[]{:S(2)}, u32[]{:S(2)}) collective-permute-start(bf16[4,256,128]{2,1,0:T(8,128)(2,1)} %copy-done.6), channel_id=1, source_target_pairs={{0,24},{4,28},{8,16},{12,20},{16,8},{20,12},{24,0},{28,4},{1,25},{... | collective-permute-start | bytes 786440 | tf_op jit(solution)/shard_map/ppermute | solution.py:200
  125.5 15.0 %collective-permute-start.13 = (bf16[4,256,128]{2,1,0:T(8,128)(2,1)}, bf16[4,256,128]{2,1,0:T(8,128)(2,1)S(1)}, u32[]{:S(2)}, u32[]{:S(2)}) collective-permute-start(bf16[4,256,128]{2,1,0:T(8,128)(2,1)} %copy-done.5), channel_id=1, source_target_pairs={{0,28},{4,24},{8,20},{12,16},{16,12},{20,8},{24,4},{28,0},{1,29},{... | collective-permute-start | bytes 786440 | tf_op jit(solution)/shard_map/ppermute | solution.py:200
  127.7 12.8 %collective-permute-start = (bf16[4,256,128]{2,1,0:T(8,128)(2,1)S(1)}, bf16[4,256,128]{2,1,0:T(8,128)(2,1)S(1)}, u32[]{:S(2)}, u32[]{:S(2)}) collective-permute-start(bf16[4,256,128]{2,1,0:T(8,128)(2,1)S(1)} %get-tuple-element.25), channel_id=1, source_target_pairs={{0,4},{4,0},{8,12},{12,8},{16,20},{20,16},{24,28},{28,24},{1,5},{5... | collective-permute-start | bytes 786440 | tf_op jit(solution)/shard_map/ppermute | solution.py:200
  127.7 16.0 %collective-permute-start.1 = (bf16[4,256,128]{2,1,0:T(8,128)(2,1)S(1)}, bf16[4,256,128]{2,1,0:T(8,128)(2,1)S(1)}, u32[]{:S(2)}, u32[]{:S(2)}) collective-permute-start(bf16[4,256,128]{2,1,0:T(8,128)(2,1)S(1)} %get-tuple-element.26), channel_id=1, source_target_pairs={{0,8},{4,12},{8,0},{12,4},{16,24},{20,28},{24,16},{28,20},{1,9},{5... | collective-permute-start | bytes 786440 | tf_op jit(solution)/shard_map/ppermute | solution.py:200
  127.8 85.0 %collective-permute-start.2 = (bf16[4,256,128]{2,1,0:T(8,128)(2,1)}, bf16[4,256,128]{2,1,0:T(8,128)(2,1)S(1)}, u32[]{:S(2)}, u32[]{:S(2)}) collective-permute-start(bf16[4,256,128]{2,1,0:T(8,128)(2,1)} %get-tuple-element.27), channel_id=1, source_target_pairs={{0,12},{4,8},{8,4},{12,0},{16,28},{20,24},{24,20},{28,16},{1,13},{... | collective-permute-start | bytes 786440 | tf_op jit(solution)/shard_map/ppermute | solution.py:200
  132.0 15.3 %copy-start.9 = (bf16[4,256,128]{2,1,0:T(8,128)(2,1)}, bf16[4,256,128]{2,1,0:T(8,128)(2,1)S(1)}, u32[]{:S(2)}) copy-start(bf16[4,256,128]{2,1,0:T(8,128)(2,1)S(1)} %collective-permute-done.12.refs_6_) | copy-start | bytes 786436
  132.0 80.9 %collective-permute-start.3 = (bf16[4,256,128]{2,1,0:T(8,128)(2,1)}, bf16[4,256,128]{2,1,0:T(8,128)(2,1)S(1)}, u32[]{:S(2)}, u32[]{:S(2)}) collective-permute-start(bf16[4,256,128]{2,1,0:T(8,128)(2,1)} %get-tuple-element.28), channel_id=1, source_target_pairs={{0,16},{4,20},{8,24},{12,28},{16,0},{20,4},{24,8},{28,12},{1,17},{... | collective-permute-start | bytes 786440 | tf_op jit(solution)/shard_map/ppermute | solution.py:200
  140.5 6.8 %copy-start.11 = (bf16[4,256,128]{2,1,0:T(8,128)(2,1)}, bf16[4,256,128]{2,1,0:T(8,128)(2,1)S(1)}, u32[]{:S(2)}) copy-start(bf16[4,256,128]{2,1,0:T(8,128)(2,1)S(1)} %collective-permute-done.13.refs_7_) | copy-start | bytes 786436
  140.5 72.4 %collective-permute-start.4 = (bf16[4,256,128]{2,1,0:T(8,128)(2,1)}, bf16[4,256,128]{2,1,0:T(8,128)(2,1)S(1)}, u32[]{:S(2)}, u32[]{:S(2)}) collective-permute-start(bf16[4,256,128]{2,1,0:T(8,128)(2,1)} %get-tuple-element.29), channel_id=1, source_target_pairs={{0,20},{4,16},{8,28},{12,24},{16,4},{20,0},{24,12},{28,8},{1,21},{... | collective-permute-start | bytes 786440 | tf_op jit(solution)/shard_map/ppermute | solution.py:200
  140.5 72.4 %copy-start.7 = (bf16[4,256,128]{2,1,0:T(8,128)(2,1)}, bf16[4,256,128]{2,1,0:T(8,128)(2,1)S(1)}, u32[]{:S(2)}) copy-start(bf16[4,256,128]{2,1,0:T(8,128)(2,1)S(1)} %collective-permute-done.refs_1_) | copy-start | bytes 786436
  140.5 72.4 %collective-permute-start.5 = (bf16[4,256,128]{2,1,0:T(8,128)(2,1)}, bf16[4,256,128]{2,1,0:T(8,128)(2,1)S(1)}, u32[]{:S(2)}, u32[]{:S(2)}) collective-permute-start(bf16[4,256,128]{2,1,0:T(8,128)(2,1)} %get-tuple-element.30), channel_id=1, source_target_pairs={{0,24},{4,28},{8,16},{12,20},{16,8},{20,12},{24,0},{28,4},{1,25},{... | collective-permute-start | bytes 786440 | tf_op jit(solution)/shard_map/ppermute | solution.py:200
  143.7 69.2 %copy-start.8 = (bf16[4,256,128]{2,1,0:T(8,128)(2,1)}, bf16[4,256,128]{2,1,0:T(8,128)(2,1)S(1)}, u32[]{:S(2)}) copy-start(bf16[4,256,128]{2,1,0:T(8,128)(2,1)S(1)} %collective-permute-done.1.refs_2_) | copy-start | bytes 786436
  143.7 69.2 %collective-permute-start.6 = (bf16[4,256,128]{2,1,0:T(8,128)(2,1)S(1)}, bf16[4,256,128]{2,1,0:T(8,128)(2,1)S(1)}, u32[]{:S(2)}, u32[]{:S(2)}) collective-permute-start(bf16[4,256,128]{2,1,0:T(8,128)(2,1)S(1)} %get-tuple-element.31), channel_id=1, source_target_pairs={{0,28},{4,24},{8,20},{12,16},{16,12},{20,8},{24,4},{28,0},{1,29},{... | collective-permute-start | bytes 786440 | tf_op jit(solution)/shard_map/ppermute | solution.py:200
  212.8 0.7 copy-start.10
  212.9 0.8 copy-start.12
  212.9 0.9 copy-start.13
  212.9 0.9 copy-start.14
  212.9 1.0 copy-start.15
  (1 other events, 0.7 us)
